TPU v7x, 32 devices: a whole 2x2x4 slice. The times are simulated.
32 devices in a mesh: replica: 2 (over x), node: 2 (over core), local: 8 (over z, y).
Axes of the slice: x: 2, y: 2, z: 4, core: 2. Of those that a mesh axis runs over, the one named last changes fastest.
Arguments:
- hidden: bfloat16 [384, 7168], P(('replica', 'node', 'local')), parts along dimension 0, may hold values from -48 to 48
- norm_gain: float32 [7168], replicated, may hold values from 0.25 to 1.75
- expert_ids: int32 [384, 2], P(('replica', 'node', 'local')), parts along dimension 0, may hold values from 0 to 7, all different within a row; in each aligned block of 12 rows (0 to 11, 12 to 23, ...) at most 4 rows name the same one
- gate_weight: float32 [384, 2], P(('replica', 'node', 'local')), parts along dimension 0, may hold values from 0.2 to 1
- gate_proj: bfloat16 [7168, 16384], P(None, ('node', 'local')), may hold values from -0.0625 to 0.0625
- up_proj: bfloat16 [7168, 16384], P(None, ('node', 'local')), may hold values from -0.0625 to 0.0625
- down_proj: bfloat16 [16384, 7168], P(('node', 'local')), may hold values from -0.125 to 0.125
Outputs:
- mixed: bfloat16 [384, 7168], P(('replica', 'node', 'local')), parts along dimension 0
There are 2 independent parts, one for each index of `replica`. A program takes and returns all parts, laid end to end along the dimension named above; an argument that names none is the same for every part. Nothing has to cross between parts.
Inputs may be any that keep to these rules, and one draw needn't show every extreme that they name: `expert_ids`: each row names 2 different experts. Within each device's block of 12 rows no expert is named by more than 4 rows, and some block reaches that.
All inputs are finite; a program needn't handle non-finite values.
Results may differ from a plain program's by a relative error of at most 0.008.
Values may be sent and summed in bfloat16 or wider, within the bound.
A program may use at most 128 MiB of HBM per device.

v0:
```python
import functools

import jax
import jax.numpy as jnp
from jax import lax
from jax.experimental import pallas as pl
from jax.experimental.pallas import tpu as pltpu
from jax.sharding import PartitionSpec as P

EXP_GROUP = 4
CAPACITY = 4
SEGS = 4
PAD_ROWS = 16
MESH = pl.DeviceIdType.MESH
F32 = jnp.float32
BF16 = jnp.bfloat16


def iota(shape, dim):
    return lax.broadcasted_iota(jnp.int32, shape, dim)


def one_hot_shuffle(experts, to_segments):
    rows = experts * SEGS * CAPACITY
    first, second = iota((rows, rows), 0), iota((rows, rows), 1)
    by_segment, by_expert = (first, second) if to_segments else (second, first)
    expert = by_expert // (SEGS * CAPACITY)
    segment = (by_expert // CAPACITY) % SEGS
    slot = by_expert % CAPACITY
    wanted = segment * (experts * CAPACITY) + expert * CAPACITY + slot
    return (by_segment == wanted).astype(F32).astype(BF16)


def kernel(
    dims,
    hidden_ref, gain_ref, ids_ref, weight_ref, gate_hbm, up_hbm, down_hbm,
    out_ref,
    gate_w, up_w, down_w, stacked, picks, mixing, outbox, inbox, rows_in, gate_acc, up_acc,
    part_out, part_in, sum_out, sum_in,
    w_sem, row_send, row_recv, fwd_send, fwd_recv, part_send, part_recv, sum_send, sum_recv,
):
    experts, sharers, chunks, width, row_count, routes = dims
    slots = SEGS * CAPACITY
    flat = experts * slots
    block = experts * CAPACITY
    model_width = hidden_ref.shape[1]
    seg_width = model_width // SEGS
    replica = lax.axis_index("replica")
    node = lax.axis_index("node")
    local = lax.axis_index("local")
    sharer = lax.rem(local, sharers)
    mine = node * EXP_GROUP + lax.div(local, sharers)

    def at_expert(expert, share):
        return (
            replica,
            lax.div(expert, EXP_GROUP),
            lax.rem(expert, EXP_GROUP) * sharers + share,
        )

    def other_expert(step):
        return lax.rem(mine + step, experts)

    def other_sharer(step):
        return lax.rem(sharer + step, sharers)

    def weight_copy(kind, chunk, seg):
        at = seg * seg_width + chunk * width
        if kind == 2:
            source = down_hbm.at[:, pl.ds(at, width)]
            target = down_w.at[chunk, :, pl.ds(seg * width, width)]
        else:
            source = (gate_hbm, up_hbm)[kind].at[pl.ds(at, width), :]
            target = (gate_w, up_w)[kind].at[chunk, pl.ds(seg * width, width), :]
        return pltpu.make_async_copy(source, target, w_sem.at[kind, chunk, seg])

    for chunk in range(chunks):
        for kind in range(2):
            for seg in range(SEGS):
                weight_copy(kind, chunk, seg).start()
    for chunk in range(chunks):
        for seg in range(SEGS):
            weight_copy(2, chunk, seg).start()

    barrier = pltpu.get_barrier_semaphore()
    for step in range(1, experts):
        pl.semaphore_signal(
            barrier, inc=1, device_id=at_expert(other_expert(step), sharer), device_id_type=MESH
        )
    for step in range(1, sharers):
        pl.semaphore_signal(
            barrier, inc=1, device_id=at_expert(mine, other_sharer(step)), device_id_type=MESH
        )

    lane_expert = iota((row_count, flat), 1) // slots
    lane_slot = iota((row_count, flat), 1) % CAPACITY
    chosen = jnp.zeros((row_count, flat), F32)
    weights = jnp.zeros((row_count, flat), F32)
    for route in range(routes):
        named = ids_ref[:, route:route + 1] == lane_expert
        chosen = jnp.where(named, 1.0, chosen)
        weights = jnp.where(named, weight_ref[:, route:route + 1], weights)
    picks[...] = jnp.zeros_like(picks)
    mixing[...] = jnp.zeros_like(mixing)
    before = jnp.zeros((1, flat), F32)
    lane_slot_f = (iota((1, flat), 1) % CAPACITY).astype(F32)
    lane_seg = (iota((1, flat), 1) // CAPACITY) % SEGS
    for row in range(row_count):
        chosen_row = chosen[row:row + 1, :]
        hit = jnp.where(before == lane_slot_f, chosen_row, 0.0)
        scaled = hit * weights[row:row + 1, :]
        for seg in range(SEGS):
            here = lane_seg == seg
            picks[pl.ds(seg * PAD_ROWS + row, 1), :] = jnp.where(here, hit, 0.0)
            mixing[pl.ds(seg * PAD_ROWS + row, 1), :] = jnp.where(here, scaled, 0.0)
        before = before + chosen_row

    values = hidden_ref[...].astype(F32)
    scale = lax.rsqrt(jnp.mean(values * values, axis=1, keepdims=True) + 1e-06)
    normed = values * scale * gain_ref[...]
    stacked[...] = jnp.zeros_like(stacked)
    for seg in range(SEGS):
        stacked[pl.ds(seg * PAD_ROWS, row_count), :] = normed[
            :, seg * seg_width:(seg + 1) * seg_width
        ]
    picked = picks[...].astype(BF16)

    def row_copy(chunk, source_expert, target_expert):
        return pltpu.make_async_remote_copy(
            src_ref=outbox.at[chunk, target_expert],
            dst_ref=inbox.at[chunk, sharer, source_expert],
            send_sem=row_send.at[chunk, target_expert],
            recv_sem=row_recv.at[chunk, source_expert],
            device_id=at_expert(target_expert, sharer),
            device_id_type=MESH,
        )

    def forward_copy(chunk, source_share, target_share):
        return pltpu.make_async_remote_copy(
            src_ref=inbox.at[chunk, source_share],
            dst_ref=inbox.at[chunk, source_share],
            send_sem=fwd_send.at[chunk, target_share],
            recv_sem=fwd_recv.at[chunk, source_share],
            device_id=at_expert(mine, target_share),
            device_id_type=MESH,
        )

    def part_copy(chunk, source_share, target_share):
        return pltpu.make_async_remote_copy(
            src_ref=part_out.at[chunk, target_share],
            dst_ref=part_in.at[chunk, source_share],
            send_sem=part_send.at[chunk, target_share],
            recv_sem=part_recv.at[chunk, source_share],
            device_id=at_expert(mine, target_share),
            device_id_type=MESH,
        )

    def sum_copy(chunk, source_expert, target_expert):
        return pltpu.make_async_remote_copy(
            src_ref=sum_out.at[chunk, target_expert],
            dst_ref=sum_in.at[chunk, source_expert],
            send_sem=sum_send.at[chunk, target_expert],
            recv_sem=sum_recv.at[chunk, source_expert],
            device_id=at_expert(target_expert, sharer),
            device_id_type=MESH,
        )

    pl.semaphore_wait(barrier, experts - 1 + sharers - 1)

    for chunk in range(chunks):
        rows = stacked[:, chunk * width:(chunk + 1) * width].astype(BF16)
        placed = lax.dot_general(
            picked, rows, (((0,), (0,)), ((), ())), preferred_element_type=F32
        ).astype(BF16)
        outbox[chunk] = placed.reshape(experts, slots, width)
        for step in range(1, experts):
            row_copy(chunk, mine, other_expert(step)).start()
        inbox[chunk, sharer, mine] = outbox[chunk, mine]

    to_segments = one_hot_shuffle(experts, True)
    to_experts = one_hot_shuffle(experts, False)

    def gather_rows(chunk):
        for step in range(1, experts):
            source = other_expert(step)
            row_copy(chunk, source, source).wait_recv()
        for step in range(1, sharers):
            forward_copy(chunk, sharer, other_sharer(step)).start()

    def expand(chunk):
        for step in range(1, sharers):
            source = other_sharer(step)
            forward_copy(chunk, source, source).wait_recv()
        for share in range(sharers):
            ordered = jnp.dot(
                to_segments,
                inbox[chunk, share].reshape(flat, width),
                preferred_element_type=F32,
            ).astype(BF16)
            for seg in range(SEGS):
                rows_in[share * block:(share + 1) * block, seg * width:(seg + 1) * width] = (
                    ordered[seg * block:(seg + 1) * block]
                )
        for kind, matrix, total in ((0, gate_w, gate_acc), (1, up_w, up_acc)):
            for seg in range(SEGS):
                weight_copy(kind, chunk, seg).wait()
            product = jnp.dot(rows_in[...], matrix[chunk], preferred_element_type=F32)
            if chunk == 0:
                total[...] = product
            else:
                total[...] += product

    for chunk in range(chunks):
        gather_rows(chunk)
        if chunk >= 1:
            expand(chunk - 1)
    expand(chunks - 1)

    gate = gate_acc[...]
    active = (gate / (1.0 + jnp.exp(-gate)) * up_acc[...]).astype(BF16)

    mix = mixing[...]
    mix_high = mix.astype(BF16)
    rest = mix - mix_high.astype(F32)
    mix_mid = rest.astype(BF16)
    mix_low = (rest - mix_mid.astype(F32)).astype(BF16)
    mix_parts = jnp.concatenate([mix_high, mix_mid, mix_low], axis=0)

    def contract(chunk):
        for seg in range(SEGS):
            weight_copy(2, chunk, seg).wait()
        product = jnp.dot(active, down_w[chunk], preferred_element_type=F32).astype(BF16)
        for share in range(sharers):
            for seg in range(SEGS):
                part_out[chunk, share, seg * block:(seg + 1) * block, :] = product[
                    share * block:(share + 1) * block, seg * width:(seg + 1) * width
                ]
        for step in range(1, sharers):
            part_copy(chunk, sharer, other_sharer(step)).start()

    def add_parts(chunk):
        total = part_out[chunk, sharer].astype(F32)
        for step in range(1, sharers):
            source = other_sharer(step)
            part_copy(chunk, source, source).wait_recv()
            total = total + part_in[chunk, source].astype(F32)
        ordered = jnp.dot(to_experts, total.astype(BF16), preferred_element_type=F32).astype(BF16)
        sum_out[chunk] = ordered.reshape(experts, slots, width)
        for step in range(1, experts):
            sum_copy(chunk, mine, other_expert(step)).start()
        sum_in[chunk, mine] = sum_out[chunk, mine]

    def mix_rows(chunk):
        for step in range(1, experts):
            source = other_expert(step)
            sum_copy(chunk, source, source).wait_recv()
        arrived = sum_in[chunk].reshape(flat, width)
        terms = jnp.dot(mix_parts, arrived, preferred_element_type=F32)
        size = SEGS * PAD_ROWS
        mixed = terms[:size] + terms[size:2 * size] + terms[2 * size:]
        for seg in range(SEGS):
            at = seg * seg_width + chunk * width
            out_ref[:, at:at + width] = mixed[
                seg * PAD_ROWS:seg * PAD_ROWS + row_count
            ].astype(BF16)

    for turn in range(chunks + 4):
        if turn < chunks:
            contract(turn)
        if 0 <= turn - 1 < chunks:
            add_parts(turn - 1)
        if 0 <= turn - 4 < chunks:
            mix_rows(turn - 4)

    for chunk in range(chunks):
        for step in range(1, experts):
            row_copy(chunk, mine, other_expert(step)).wait_send()
            sum_copy(chunk, mine, other_expert(step)).wait_send()
        for step in range(1, sharers):
            forward_copy(chunk, sharer, other_sharer(step)).wait_send()
            part_copy(chunk, sharer, other_sharer(step)).wait_send()


def shards(hidden, norm_gain, expert_ids, gate_weight, gate_proj, up_proj, down_proj):
    experts = EXP_GROUP * lax.axis_size("node")
    sharers = lax.axis_size("local") // EXP_GROUP
    row_count, model_width = hidden.shape
    routes = expert_ids.shape[1]
    units = gate_proj.shape[1]
    seg_width = model_width // SEGS
    width = 256
    chunks = seg_width // width
    slots = SEGS * CAPACITY
    flat = experts * slots
    block = experts * CAPACITY
    vmem = pl.BlockSpec(memory_space=pltpu.VMEM)
    anywhere = pl.BlockSpec(memory_space=pl.ANY)
    dma = pltpu.SemaphoreType.DMA
    return pl.pallas_call(
        functools.partial(kernel, (experts, sharers, chunks, width, row_count, routes)),
        out_shape=jax.ShapeDtypeStruct((row_count, model_width), BF16),
        in_specs=[vmem] * 4 + [anywhere] * 3,
        out_specs=vmem,
        scratch_shapes=[
            pltpu.VMEM((chunks, SEGS * width, units), BF16),
            pltpu.VMEM((chunks, SEGS * width, units), BF16),
            pltpu.VMEM((chunks, units, SEGS * width), BF16),
            pltpu.VMEM((SEGS * PAD_ROWS, seg_width), F32),
            pltpu.VMEM((SEGS * PAD_ROWS, flat), F32),
            pltpu.VMEM((SEGS * PAD_ROWS, flat), F32),
            pltpu.VMEM((chunks, experts, slots, width), BF16),
            pltpu.VMEM((chunks, sharers, experts, slots, width), BF16),
            pltpu.VMEM((sharers * block, SEGS * width), BF16),
            pltpu.VMEM((sharers * block, units), F32),
            pltpu.VMEM((sharers * block, units), F32),
            pltpu.VMEM((chunks, sharers, SEGS * block, width), BF16),
            pltpu.VMEM((chunks, sharers, SEGS * block, width), BF16),
            pltpu.VMEM((chunks, experts, slots, width), BF16),
            pltpu.VMEM((chunks, experts, slots, width), BF16),
            dma((3, chunks, SEGS)),
            dma((chunks, experts)),
            dma((chunks, experts)),
            dma((chunks, sharers)),
            dma((chunks, sharers)),
            dma((chunks, sharers)),
            dma((chunks, sharers)),
            dma((chunks, experts)),
            dma((chunks, experts)),
        ],
        compiler_params=pltpu.CompilerParams(
            collective_id=0, has_side_effects=True, vmem_limit_bytes=58 * 1024 * 1024
        ),
        name="expert_layer",
    )(hidden, norm_gain.reshape(1, model_width), expert_ids, gate_weight, gate_proj, up_proj, down_proj)


def solution(mesh):
    return jax.shard_map(
        shards,
        mesh=mesh,
        in_specs=(
            P(("replica", "node", "local"), None),
            P(),
            P(("replica", "node", "local"), None),
            P(("replica", "node", "local"), None),
            P(None, ("node", "local")),
            P(None, ("node", "local")),
            P(("node", "local"), None),
        ),
        out_specs=P(("replica", "node", "local"), None),
        check_vma=False,
    )
```

profile of v0, /device:TPU:0, one launch (start us, length us, event | category | flops | bytes accessed | tf_op | source)
XLA Modules:
  0.0 57.9 jit_solution(2214876652139672780)
XLA Ops:
  0.0 1.4 %copy.8.ids_ref = s32[12,2]{1,0:T(8,128)} copy(s32[12,2]{0,1:T(2,128)} %param.9) | data formatting | bytes 192 | tf_op args[2]
  1.4 1.4 %copy.9.weight_ref = f32[12,2]{1,0:T(8,128)} copy(f32[12,2]{0,1:T(2,128)} %param.10) | data formatting | bytes 192 | tf_op args[3]
  2.7 53.5 %expert_layer.1 = bf16[12,7168]{1,0:T(8,128)(2,1)} custom-call(bf16[12,7168]{1,0:T(8,128)(2,1)} %hidden_ref.1, f32[1,7168]{1,0:T(1,128)} %bitcast.1, s32[12,2]{1,0:T(8,128)} %copy.8.ids_ref, f32[12,2]{1,0:T(8,128)} %copy.9.weight_ref, bf16[7168,1024]{1,0:T(8,128)(2,1)} %gate_hbm.1, bf16[7168,1024]{1,0:T(8,128)(2,1)} %up_hbm.1, bf16[1024,7168]{1,0:T(8,128)(2,1)} %down_hbm.1), custom_call_target="tpu_custom_call" | custom-call | tf_op jit(solution)/shard_map/expert_layer/pallas_call | solution.py:299
  56.2 1.6 %copy.11 = bf16[12,7168]{1,0:T(8,128)(2,1)} copy(bf16[12,7168]{1,0:T(8,128)(2,1)} %expert_layer.1) | data formatting | bytes 344064
where the time goes:
time: 58 us; the launch traced here: 57.9 us
  Pallas kernels  53.5 us (92%)
  local copies, waits for them, and re-layouts  4.36 us (8%)
    pallas_call x1, Pallas kernels, shards(): pl.pallas_call(functools.partial(kernel, (experts, sharers, chunks, width...  53.5 us
    unnamed x3, local copies, waits for them, and re-layouts  4.36 us

commit v1 on v0

v1 whole, which is shorter than its diff:
```python
import functools

import jax
import jax.numpy as jnp
from jax import lax
from jax.experimental import pallas as pl
from jax.experimental.pallas import tpu as pltpu
from jax.sharding import PartitionSpec as P

EXP_GROUP = 4
CAPACITY = 4
SEGS = 4
PAD_ROWS = 16
IN_FLIGHT = 2
ADD_LAG = 2
MIX_LAG = 4
ROW_CUTS = (7, 7)
OUT_CUTS = (4, 4, 4, 2)
MESH = pl.DeviceIdType.MESH
F32 = jnp.float32
BF16 = jnp.bfloat16


def iota(shape, dim):
    return lax.broadcasted_iota(jnp.int32, shape, dim)


def spans(cuts, whole):
    unit, at, out = whole // sum(cuts), 0, []
    for cut in cuts:
        out.append((at, cut * unit))
        at += cut * unit
    return out


def one_hot_shuffle(experts, to_segments):
    rows = experts * SEGS * CAPACITY
    first, second = iota((rows, rows), 0), iota((rows, rows), 1)
    by_segment, by_expert = (first, second) if to_segments else (second, first)
    expert = by_expert // (SEGS * CAPACITY)
    segment = (by_expert // CAPACITY) % SEGS
    slot = by_expert % CAPACITY
    wanted = segment * (experts * CAPACITY) + expert * CAPACITY + slot
    return (by_segment == wanted).astype(F32).astype(BF16)


def kernel(
    dims,
    hidden_ref, gain_ref, ids_ref, weight_ref, gate_hbm, up_hbm, down_hbm,
    out_ref,
    gate_w, up_w, down_w, stacked, mixing, outbox, inbox, rows_in, gate_acc, up_acc,
    part_out, part_in, sum_out, sum_in,
    w_sem, row_send, row_recv, fwd_send, part_send, part_recv, sum_send, sum_recv,
):
    experts, sharers, row_count, routes = dims
    slots = SEGS * CAPACITY
    flat = experts * slots
    block = experts * CAPACITY
    model_width = hidden_ref.shape[1]
    seg_width = model_width // SEGS
    row_spans, out_spans = spans(ROW_CUTS, seg_width), spans(OUT_CUTS, seg_width)
    nodes = experts // EXP_GROUP
    replica = lax.axis_index("replica")
    node = lax.axis_index("node")
    local = lax.axis_index("local")
    sharer = lax.rem(local, sharers)
    mine = node * EXP_GROUP + lax.div(local, sharers)

    def at_expert(expert, share):
        return (
            replica,
            lax.div(expert, EXP_GROUP),
            lax.rem(expert, EXP_GROUP) * sharers + share,
        )

    def other_expert(step):
        return lax.rem(mine + step + experts, experts)

    away = [step for step in range(1, experts) if step % EXP_GROUP]
    away.sort(key=lambda step: min(step % EXP_GROUP, -step % EXP_GROUP))
    here = [step for step in range(EXP_GROUP, experts, EXP_GROUP)]

    def other_sharer(step):
        return lax.rem(sharer + step, sharers)

    def weight_copy(kind, chunk, seg):
        offset, width = (out_spans if kind == 2 else row_spans)[chunk]
        held = pl.ds(SEGS * offset + seg * width, width)
        taken = pl.ds(seg * seg_width + offset, width)
        if kind == 2:
            source, target = down_hbm.at[:, taken], down_w.at[:, held]
        else:
            source = (gate_hbm, up_hbm)[kind].at[taken, :]
            target = (gate_w, up_w)[kind].at[held, :]
        return pltpu.make_async_copy(source, target, w_sem.at[kind, chunk, seg])

    for chunk in range(len(row_spans)):
        for kind in range(2):
            for seg in range(SEGS):
                weight_copy(kind, chunk, seg).start()
    for chunk in range(len(out_spans)):
        for seg in range(SEGS):
            weight_copy(2, chunk, seg).start()

    barrier = pltpu.get_barrier_semaphore()
    for step in range(1, experts):
        pl.semaphore_signal(
            barrier, inc=1, device_id=at_expert(other_expert(step), sharer), device_id_type=MESH
        )
    for step in range(1, sharers):
        pl.semaphore_signal(
            barrier, inc=1, device_id=at_expert(mine, other_sharer(step)), device_id_type=MESH
        )
        for ahead in here:
            pl.semaphore_signal(
                barrier,
                inc=1,
                device_id=at_expert(other_expert(ahead), other_sharer(step)),
                device_id_type=MESH,
            )

    shape = (flat, 2 * SEGS * PAD_ROWS)
    lanes = shape[1]
    spread = (iota((row_count, lanes), 0) == iota((row_count, lanes), 1) % PAD_ROWS).astype(F32)
    named = jnp.dot(ids_ref[...].astype(F32), spread, preferred_element_type=F32)
    shares = jnp.dot(
        weight_ref[...], spread, precision=lax.Precision.HIGHEST, preferred_element_type=F32
    )
    expert = (iota(shape, 0) // slots).astype(F32)
    lane_row = iota(shape, 1) % PAD_ROWS
    chosen = jnp.zeros(shape, F32)
    weights = jnp.zeros(shape, F32)
    for route in range(routes):
        same = (named[route:route + 1, :] == expert) & (lane_row < row_count)
        chosen = jnp.where(same, 1.0, chosen)
        weights = jnp.where(same, shares[route:route + 1, :], weights)
    first, second = iota((lanes, lanes), 0), iota((lanes, lanes), 1)
    earlier = (first // PAD_ROWS == second // PAD_ROWS) & (first < second)
    before = jnp.dot(
        chosen.astype(BF16), earlier.astype(F32).astype(BF16), preferred_element_type=F32
    )
    same_seg = (iota(shape, 0) // CAPACITY) % SEGS == iota(shape, 1) // PAD_ROWS
    fills = (before == (iota(shape, 0) % CAPACITY).astype(F32)) & same_seg
    hit = jnp.where(fills, chosen, 0.0)
    mixing[...] = jnp.where(fills, weights, 0.0)
    picked = hit.astype(BF16)[:, :SEGS * PAD_ROWS]

    values = hidden_ref[...].astype(F32)
    scale = lax.rsqrt(jnp.mean(values * values, axis=1, keepdims=True) + 1e-06)
    normed = values * scale * gain_ref[...]
    stacked[...] = jnp.zeros_like(stacked)
    for seg in range(SEGS):
        stacked[pl.ds(seg * PAD_ROWS, row_count), :] = normed[
            :, seg * seg_width:(seg + 1) * seg_width
        ]

    def columns(span):
        return pl.ds(span[0], span[1])

    def row_copy(chunk, source_expert, target_expert, source_share, target_share):
        span = columns(row_spans[chunk])
        return pltpu.make_async_remote_copy(
            src_ref=outbox.at[target_expert, :, span],
            dst_ref=inbox.at[source_share, source_expert, :, span],
            send_sem=row_send.at[chunk, target_share, target_expert],
            recv_sem=row_recv.at[chunk, source_share, source_expert],
            device_id=at_expert(target_expert, target_share),
            device_id_type=MESH,
        )

    def forward_copy(chunk, source_expert, target_share):
        span = columns(row_spans[chunk])
        return pltpu.make_async_remote_copy(
            src_ref=inbox.at[sharer, source_expert, :, span],
            dst_ref=inbox.at[sharer, source_expert, :, span],
            send_sem=fwd_send.at[chunk, target_share, source_expert],
            recv_sem=row_recv.at[chunk, sharer, source_expert],
            device_id=at_expert(mine, target_share),
            device_id_type=MESH,
        )

    def part_copy(chunk, source_share, target_share):
        return pltpu.make_async_remote_copy(
            src_ref=part_out.at[target_share, :, columns(out_spans[chunk])],
            dst_ref=part_in.at[source_share, :, columns(out_spans[chunk])],
            send_sem=part_send.at[chunk, target_share],
            recv_sem=part_recv.at[chunk, source_share],
            device_id=at_expert(mine, target_share),
            device_id_type=MESH,
        )

    def sum_copy(chunk, source_expert, target_expert):
        return pltpu.make_async_remote_copy(
            src_ref=sum_out.at[target_expert, :, columns(out_spans[chunk])],
            dst_ref=sum_in.at[source_expert, :, columns(out_spans[chunk])],
            send_sem=sum_send.at[chunk, target_expert],
            recv_sem=sum_recv.at[chunk, source_expert],
            device_id=at_expert(target_expert, sharer),
            device_id_type=MESH,
        )

    pl.semaphore_wait(barrier, experts - 1 + nodes * (sharers - 1))

    def place(chunk):
        offset, width = row_spans[chunk]
        rows = stacked[:, offset:offset + width].astype(BF16)
        placed = jnp.dot(picked, rows, preferred_element_type=F32).astype(BF16)
        outbox[:, :, offset:offset + width] = placed.reshape(experts, slots, width)
        for step in away:
            row_copy(chunk, mine, other_expert(step), sharer, sharer).start()
        for turn in range(1, sharers):
            row_copy(chunk, mine, mine, sharer, other_sharer(turn)).start()
            for step in here:
                row_copy(chunk, mine, other_expert(step), sharer, other_sharer(turn)).start()
        for step in here:
            row_copy(chunk, mine, other_expert(step), sharer, sharer).start()
        inbox[sharer, mine, :, offset:offset + width] = outbox[mine, :, offset:offset + width]

    to_segments = one_hot_shuffle(experts, True)
    to_experts = one_hot_shuffle(experts, False)

    def arrive(chunk, source, share):
        row_copy(chunk, source, source, share, share).wait_recv()

    def gather_rows(chunk):
        for step in away:
            source = other_expert(-step)
            arrive(chunk, source, sharer)
            for turn in range(1, sharers):
                forward_copy(chunk, source, other_sharer(turn)).start()
        for step in here:
            arrive(chunk, other_expert(-step), sharer)

    def expand(chunk):
        offset, width = row_spans[chunk]
        for turn in range(1, sharers):
            for source in range(experts):
                arrive(chunk, source, other_sharer(turn))
        for share in range(sharers):
            ordered = jnp.dot(
                to_segments,
                inbox[share, :, :, offset:offset + width].reshape(flat, width),
                preferred_element_type=F32,
            ).astype(BF16)
            for seg in range(SEGS):
                at = SEGS * offset + seg * width
                rows_in[share * block:(share + 1) * block, at:at + width] = (
                    ordered[seg * block:(seg + 1) * block]
                )
        held = slice(SEGS * offset, SEGS * (offset + width))
        for kind, matrix, total in ((0, gate_w, gate_acc), (1, up_w, up_acc)):
            for seg in range(SEGS):
                weight_copy(kind, chunk, seg).wait()
            product = jnp.dot(rows_in[:, held], matrix[held], preferred_element_type=F32)
            if chunk == 0:
                total[...] = product
            else:
                total[...] += product

    for chunk in range(len(row_spans)):
        place(chunk)
    for chunk in range(len(row_spans)):
        gather_rows(chunk)
        if chunk >= 1:
            expand(chunk - 1)
    expand(len(row_spans) - 1)

    gate = gate_acc[...]
    active = (gate / (1.0 + jnp.exp(-gate)) * up_acc[...]).astype(BF16)

    mix = jnp.transpose(mixing[...])[:SEGS * PAD_ROWS]
    mix_high = mix.astype(BF16)
    rest = mix - mix_high.astype(F32)
    mix_mid = rest.astype(BF16)
    mix_low = (rest - mix_mid.astype(F32)).astype(BF16)
    mix_parts = jnp.concatenate([mix_high, mix_mid, mix_low], axis=0)

    def contract(chunk):
        offset, width = out_spans[chunk]
        for seg in range(SEGS):
            weight_copy(2, chunk, seg).wait()
        product = jnp.dot(
            active,
            down_w[:, SEGS * offset:SEGS * (offset + width)],
            preferred_element_type=F32,
        ).astype(BF16)
        for share in range(sharers):
            for seg in range(SEGS):
                part_out[share, seg * block:(seg + 1) * block, offset:offset + width] = product[
                    share * block:(share + 1) * block, seg * width:(seg + 1) * width
                ]
        for step in range(1, sharers):
            if chunk >= IN_FLIGHT:
                part_copy(chunk - IN_FLIGHT, sharer, other_sharer(step)).wait_send()
            part_copy(chunk, sharer, other_sharer(step)).start()

    def add_parts(chunk):
        offset, width = out_spans[chunk]
        total = part_out[sharer, :, offset:offset + width].astype(F32)
        for step in range(1, sharers):
            source = other_sharer(step)
            part_copy(chunk, source, source).wait_recv()
            total = total + part_in[source, :, offset:offset + width].astype(F32)
        ordered = jnp.dot(to_experts, total.astype(BF16), preferred_element_type=F32).astype(BF16)
        sum_out[:, :, offset:offset + width] = ordered.reshape(experts, slots, width)
        for step in away + here:
            sum_copy(chunk, mine, other_expert(step)).start()
        sum_in[mine, :, offset:offset + width] = sum_out[mine, :, offset:offset + width]

    def mix_rows(chunk):
        offset, width = out_spans[chunk]
        for step in away + here:
            source = other_expert(-step)
            sum_copy(chunk, source, source).wait_recv()
        arrived = sum_in[:, :, offset:offset + width].reshape(flat, width)
        terms = jnp.dot(mix_parts, arrived, preferred_element_type=F32)
        size = SEGS * PAD_ROWS
        mixed = terms[:size] + terms[size:2 * size] + terms[2 * size:]
        for seg in range(SEGS):
            at = seg * seg_width + offset
            out_ref[:, at:at + width] = mixed[
                seg * PAD_ROWS:seg * PAD_ROWS + row_count
            ].astype(BF16)

    count = len(out_spans)
    for turn in range(count + MIX_LAG):
        if turn < count:
            contract(turn)
        if 0 <= turn - ADD_LAG < count:
            add_parts(turn - ADD_LAG)
        if 0 <= turn - MIX_LAG < count:
            mix_rows(turn - MIX_LAG)

    for chunk in range(len(row_spans)):
        for step in away + here:
            row_copy(chunk, mine, other_expert(step), sharer, sharer).wait_send()
        for turn in range(1, sharers):
            share = other_sharer(turn)
            for step in [0] + here:
                row_copy(chunk, mine, other_expert(step), sharer, share).wait_send()
            for step in away:
                forward_copy(chunk, other_expert(-step), share).wait_send()
    for chunk in range(count):
        for step in away + here:
            sum_copy(chunk, mine, other_expert(step)).wait_send()
        if chunk >= count - IN_FLIGHT:
            for step in range(1, sharers):
                part_copy(chunk, sharer, other_sharer(step)).wait_send()


def shards(hidden, norm_gain, expert_ids, gate_weight, gate_proj, up_proj, down_proj):
    experts = EXP_GROUP * lax.axis_size("node")
    sharers = lax.axis_size("local") // EXP_GROUP
    row_count, model_width = hidden.shape
    routes = expert_ids.shape[1]
    units = gate_proj.shape[1]
    seg_width = model_width // SEGS
    row_chunks, out_chunks = len(ROW_CUTS), len(OUT_CUTS)
    slots = SEGS * CAPACITY
    flat = experts * slots
    block = experts * CAPACITY
    vmem = pl.BlockSpec(memory_space=pltpu.VMEM)
    anywhere = pl.BlockSpec(memory_space=pl.ANY)
    dma = pltpu.SemaphoreType.DMA
    return pl.pallas_call(
        functools.partial(kernel, (experts, sharers, row_count, routes)),
        out_shape=jax.ShapeDtypeStruct((row_count, model_width), BF16),
        in_specs=[vmem] * 4 + [anywhere] * 3,
        out_specs=vmem,
        scratch_shapes=[
            pltpu.VMEM((model_width, units), BF16),
            pltpu.VMEM((model_width, units), BF16),
            pltpu.VMEM((units, model_width), BF16),
            pltpu.VMEM((SEGS * PAD_ROWS, seg_width), F32),
            pltpu.VMEM((flat, 2 * SEGS * PAD_ROWS), F32),
            pltpu.VMEM((experts, slots, seg_width), BF16),
            pltpu.VMEM((sharers, experts, slots, seg_width), BF16),
            pltpu.VMEM((sharers * block, model_width), BF16),
            pltpu.VMEM((sharers * block, units), F32),
            pltpu.VMEM((sharers * block, units), F32),
            pltpu.VMEM((sharers, SEGS * block, seg_width), BF16),
            pltpu.VMEM((sharers, SEGS * block, seg_width), BF16),
            pltpu.VMEM((experts, slots, seg_width), BF16),
            pltpu.VMEM((experts, slots, seg_width), BF16),
            dma((3, max(row_chunks, out_chunks), SEGS)),
            dma((row_chunks, sharers, experts)),
            dma((row_chunks, sharers, experts)),
            dma((row_chunks, sharers, experts)),
            dma((out_chunks, sharers)),
            dma((out_chunks, sharers)),
            dma((out_chunks, experts)),
            dma((out_chunks, experts)),
        ],
        compiler_params=pltpu.CompilerParams(
            collective_id=0, has_side_effects=True, vmem_limit_bytes=58 * 1024 * 1024
        ),
        name="expert_layer",
    )(hidden, norm_gain.reshape(1, model_width), expert_ids.T, gate_weight.T, gate_proj, up_proj, down_proj)


def solution(mesh):
    return jax.shard_map(
        shards,
        mesh=mesh,
        in_specs=(
            P(("replica", "node", "local"), None),
            P(),
            P(("replica", "node", "local"), None),
            P(("replica", "node", "local"), None),
            P(None, ("node", "local")),
            P(None, ("node", "local")),
            P(("node", "local"), None),
        ),
        out_specs=P(("replica", "node", "local"), None),
        check_vma=False,
    )
```

time: 58 us -> 46.7 us (0.81)
  Pallas kernels: 53.5 us -> 44.9 us
  local copies, waits for them, and re-layouts: 4.36 us -> 1.64 us
    pallas_call x1, Pallas kernels: 53.5 us -> 44.9 us  [shards(): pl.pallas_call(functools.partial(kernel, (experts, sharers, row_count, ro...]
    unnamed x3 -> x1, local copies, waits for them, and re-layouts: 4.36 us -> 1.64 us
where the time goes in v1:
time: 46.7 us; the launch traced here: 46.5 us
  Pallas kernels  44.9 us (96%)
  local copies, waits for them, and re-layouts  1.64 us (4%)
    pallas_call x1, Pallas kernels, shards(): pl.pallas_call(functools.partial(kernel, (experts, sharers, row_count, ro...  44.9 us
    unnamed x1, local copies, waits for them, and re-layouts  1.64 us

profile of v1, /device:TPU:0, one launch (start us, length us, event | category | flops | bytes accessed | tf_op | source)
XLA Modules:
  0.0 46.5 jit_solution(6767626197703126840)
XLA Ops:
  0.0 44.9 %expert_layer.1 = bf16[12,7168]{1,0:T(8,128)(2,1)} custom-call(bf16[12,7168]{1,0:T(8,128)(2,1)} %hidden_ref.1, f32[1,7168]{1,0:T(1,128)} %bitcast.3, s32[2,12]{1,0:T(2,128)} %bitcast.4, f32[2,12]{1,0:T(2,128)} %bitcast.5, bf16[7168,1024]{1,0:T(8,128)(2,1)} %gate_hbm.1, bf16[7168,1024]{1,0:T(8,128)(2,1)} %up_hbm.1, bf16[1024,7168]{1,0:T(8,128)(2,1)} %down_hbm.1), custom_call_target="tpu_custom_call" | custom-call | tf_op jit(solution)/shard_map/expert_layer/pallas_call | solution.py:365
  44.9 1.6 %copy.9 = bf16[12,7168]{1,0:T(8,128)(2,1)} copy(bf16[12,7168]{1,0:T(8,128)(2,1)} %expert_layer.1) | data formatting | bytes 344064

commit v2 on v1

--- a/solution.py
+++ b/solution.py
@@ -14,7 +14,7 @@
 IN_FLIGHT = 2
 ADD_LAG = 2
 MIX_LAG = 4
-ROW_CUTS = (7, 7)
+ROW_CUTS = (9, 5)
 OUT_CUTS = (4, 4, 4, 2)
 MESH = pl.DeviceIdType.MESH
 F32 = jnp.float32

time: 46.7 us -> 46.8 us (level)
  no operation moved by 1% of the time
where the time goes in v2:
time: 46.8 us; the launch traced here: 46.7 us
  Pallas kernels  45 us (96%)
  local copies, waits for them, and re-layouts  1.64 us (4%)
    pallas_call x1, Pallas kernels, shards(): pl.pallas_call(functools.partial(kernel, (experts, sharers, row_count, ro...  45 us
    unnamed x1, local copies, waits for them, and re-layouts  1.64 us

profile of v2, /device:TPU:0, one launch (start us, length us, event | category | flops | bytes accessed | tf_op | source)
XLA Modules:
  0.0 46.7 jit_solution(9491315586786639201)
XLA Ops:
  0.0 45.0 %expert_layer.1 = bf16[12,7168]{1,0:T(8,128)(2,1)} custom-call(bf16[12,7168]{1,0:T(8,128)(2,1)} %hidden_ref.1, f32[1,7168]{1,0:T(1,128)} %bitcast.3, s32[2,12]{1,0:T(2,128)} %bitcast.4, f32[2,12]{1,0:T(2,128)} %bitcast.5, bf16[7168,1024]{1,0:T(8,128)(2,1)} %gate_hbm.1, bf16[7168,1024]{1,0:T(8,128)(2,1)} %up_hbm.1, bf16[1024,7168]{1,0:T(8,128)(2,1)} %down_hbm.1), custom_call_target="tpu_custom_call" | custom-call | tf_op jit(solution)/shard_map/expert_layer/pallas_call | solution.py:365
  45.0 1.6 %copy.9 = bf16[12,7168]{1,0:T(8,128)(2,1)} copy(bf16[12,7168]{1,0:T(8,128)(2,1)} %expert_layer.1) | data formatting | bytes 344064
